TPU v7x, 32 devices: a whole 2x2x4 slice. The times are simulated.
32 devices in a mesh: section: 4 (over x, core), dp: 8 (over z, y).
Axes of the slice: x: 2, y: 2, z: 4, core: 2. Of those that a mesh axis runs over, the one named last changes fastest.
Arguments:
- section_inputs: bfloat16 [4, 4, 256, 8192], P('section', None, 'dp'), may hold values from -6 to 6
- adapter_down: bfloat16 [4, 8192, 128], P('section'), may hold values from -0.0625 to 0.0625
- adapter_up: bfloat16 [4, 8192, 128], P('section'), may hold values from -0.5 to 0.5
- representation: bfloat16 [4, 256, 8192], P('section', 'dp'), may hold values from -6 to 6
- head_weights: bfloat16 [8192, 128], P('dp'), may hold values from -1 to 1
- head_targets: bfloat16 [4, 256, 128], P('section', 'dp'), may hold values from -40 to 40
- head_task: int32 [8, 1], replicated, may hold values from 0 to 5
Outputs:
- down_grads: float32 [4, 8192, 128], P('section', 'dp')
- up_grads: float32 [4, 8192, 128], P('section', 'dp')
- task_weights: float32 [6], replicated
Inputs may be any that keep to these rules, and one draw needn't show every extreme that they name: `head_task`: each head belongs to one task, and every task has at least one head.
All inputs are finite; a program needn't handle non-finite values.
Results may differ from a plain program's by a relative error of at most 0.022.
Values may be sent and summed in bfloat16 or wider, within the bound.
A program may use at most 64 MiB of HBM per device.

v0:
```python
import jax
import jax.numpy as jnp
from jax import lax
from jax.sharding import PartitionSpec as P

HEAD_OUT = 16
TASKS = 6
STEPS = 20


STEP_RATE = 3.0


def from_behind(value, axis, steps):
    count = lax.axis_size(axis)
    first, last = (max(0, -steps), min(count, count - steps))
    return lax.ppermute(value, axis, [(source, source + steps) for source in range(first, last)])


def swish_slope(preact):
    logistic = jax.nn.sigmoid(preact)
    return logistic * (1.0 + preact * (1.0 - logistic))


def section_back(inputs, down_map, up_map, cotangent):
    preact = jnp.dot(inputs, down_map, preferred_element_type=jnp.float32)
    active = jax.nn.silu(preact).astype(jnp.bfloat16)
    branch = jnp.dot(cotangent, up_map, preferred_element_type=jnp.float32)
    inner = (branch * swish_slope(preact)).astype(jnp.bfloat16)
    back = lax.dot_general(
        inner, down_map, (((1,), (1,)), ((), ())), preferred_element_type=jnp.float32
    )
    passed = (cotangent.astype(jnp.float32) + back).astype(jnp.bfloat16)
    return (active, inner, passed)


def store_row(buffer, value, index, valid):
    previous = lax.dynamic_index_in_dim(buffer, index, 0, keepdims=False)
    chosen = jnp.where(valid, value, previous)
    return lax.dynamic_update_index_in_dim(buffer, chosen, index, 0)


def descend(gram_matrix):
    trace_sum = jnp.trace(gram_matrix) + 1e-06
    start = jnp.full((TASKS,), 1.0 / TASKS, dtype=jnp.float32)

    def advance(counter, weights):
        descent = jnp.dot(gram_matrix, weights, precision=lax.Precision.HIGHEST) / trace_sum
        weights = weights * jnp.exp(-STEP_RATE * descent)
        return weights / jnp.sum(weights)

    return lax.fori_loop(0, STEPS, advance, start)


def body(
    section_inputs, adapter_down, adapter_up, representation, head_weights, head_targets, head_task
):
    sections = lax.axis_size("section")
    my_section = lax.axis_index("section")
    micro_count = section_inputs.shape[1]
    tok_rows = section_inputs.shape[2]
    dim_model = section_inputs.shape[3]
    rank_width = adapter_down.shape[2]
    saved = section_inputs[0]
    down_map = adapter_down[0]
    up_map = adapter_up[0]
    weights = lax.all_gather(head_weights, "dp", axis=0, tiled=True)
    predicted = jnp.dot(representation[0], weights, preferred_element_type=jnp.float32)
    residual = (predicted - head_targets[0].astype(jnp.float32)).astype(jnp.bfloat16)
    column_task = jnp.repeat(head_task[:, 0], HEAD_OUT)
    onehot = (column_task[None, :] == jnp.arange(TASKS, dtype=jnp.int32)[:, None]).astype(
        jnp.float32
    )
    masked = residual[None, :, :] * onehot.astype(jnp.bfloat16)[:, None, :]
    crossed = lax.dot_general(
        weights, weights, (((0,), (0,)), ((), ())), preferred_element_type=jnp.float32
    )
    masked_wide = masked.astype(jnp.float32)
    left_side = jnp.einsum("atc,ce->ate", masked_wide, crossed, precision=lax.Precision.HIGHEST)
    partial_gram = jnp.einsum(
        "ate,bte->ab", left_side, masked_wide, precision=lax.Precision.HIGHEST
    )
    gram_matrix = lax.psum(partial_gram, ("section", "dp"))
    mixing = descend(gram_matrix)
    column_weight = jnp.dot(mixing, onehot, precision=lax.Precision.HIGHEST)
    weighted = (residual.astype(jnp.float32) * column_weight[None, :]).astype(jnp.bfloat16)
    own_grad = jnp.einsum(
        "tc,dc->td", weighted, weights, preferred_element_type=jnp.float32
    ).astype(jnp.bfloat16)
    cotangents = lax.all_gather(own_grad[None], "section", axis=0, tiled=True)

    def tick(counter, carry):
        incoming, grad_rows, active_rows, inner_rows = carry
        micro_index = counter - (sections - 1 - my_section)
        valid = (micro_index >= 0) & (micro_index < micro_count)
        clipped = jnp.clip(micro_index, 0, micro_count - 1)
        from_heads = lax.dynamic_index_in_dim(cotangents, clipped, 0, keepdims=False)
        current = jnp.where(my_section == sections - 1, from_heads, incoming)
        inputs = lax.dynamic_index_in_dim(saved, clipped, 0, keepdims=False)
        active, inner, passed = section_back(inputs, down_map, up_map, current)
        grad_rows = store_row(grad_rows, current, clipped, valid)
        active_rows = store_row(active_rows, active, clipped, valid)
        inner_rows = store_row(inner_rows, inner, clipped, valid)
        incoming = from_behind(passed, "section", -1)
        return (incoming, grad_rows, active_rows, inner_rows)

    start_carry = (
        jnp.zeros((tok_rows, dim_model), jnp.bfloat16),
        jnp.zeros((micro_count, tok_rows, dim_model), jnp.bfloat16),
        jnp.zeros((micro_count, tok_rows, rank_width), jnp.bfloat16),
        jnp.zeros((micro_count, tok_rows, rank_width), jnp.bfloat16),
    )
    finished = lax.fori_loop(0, micro_count + sections - 1, tick, start_carry)
    grad_rows = finished[1]
    active_rows = finished[2]
    inner_rows = finished[3]
    part_down = jnp.einsum("mtd,mtr->dr", saved, inner_rows, preferred_element_type=jnp.float32)
    part_up = jnp.einsum("mtd,mtr->dr", grad_rows, active_rows, preferred_element_type=jnp.float32)
    shares = lax.psum_scatter(
        jnp.concatenate([part_down, part_up], axis=1).astype(jnp.bfloat16),
        "dp",
        scatter_dimension=0,
        tiled=True,
    ).astype(jnp.float32)
    grad_down = shares[:, :rank_width]
    grad_up = shares[:, rank_width:]
    return (grad_down[None], grad_up[None], mixing)


def solution(mesh):
    in_specs = (
        P("section", None, "dp", None),
        P("section", None, None),
        P("section", None, None),
        P("section", "dp", None),
        P("dp", None),
        P("section", "dp", None),
        P(),
    )
    out_specs = (P("section", "dp", None), P("section", "dp", None), P())
    return jax.shard_map(body, mesh=mesh, in_specs=in_specs, out_specs=out_specs, check_vma=False)
```

profile of v0, /device:TPU:0, one launch (start us, length us, event | category | flops | bytes accessed | tf_op | source)
XLA Modules:
  0.0 388.1 jit_solution(11941101329858983082)
XLA Ops:
  8.8 53.4 %all-gather.4.cloned.1.call-done = bf16[8192,128]{1,0:T(8,128)(2,1)} async-done(((bf16[1024,128]{1,0:T(8,128)(2,1)}), bf16[8192,128]{1,0:T(8,128)(2,1)}) %all-gather.4.cloned.1.call-update) | async-done | bytes 2097168 | tf_op jit(solution)/shard_map/all_gather | solution.py:67
  62.2 2.2 fusion.17
  65.6 39.3 %psum.7 = f32[6,6]{1,0:T(8,128)S(1)} all-reduce(f32[6,6]{1,0:T(8,128)S(1)} %convolution_bitcast_fusion.4), channel_id=1, replica_groups=mesh['section'=4,'dp'=8] {'section','dp'}, use_global_device_ids=true, to_apply=%region_0.0 | all-reduce | flops 36 | bytes 288 | tf_op jit(solution)/shard_map/psum | solution.py:83
  106.1 28.4 %while.33 = (s32[]{:T(128)}, f32[6]{0:T(128)S(1)}, f32[6,6]{1,0:T(8,128)S(1)}, f32[]{:T(128)}, s32[]{:T(128)}, /*index=5*/s32[]{:T(128)}) while((s32[]{:T(128)}, f32[6]{0:T(128)S(1)}, f32[6,6]{1,0:T(8,128)S(1)}, f32[]{:T(128)}, s32[]{:T(128)}, /*index=5*/s32[]{:T(128)}) %tuple.73), condition=%wide.region_4.5_spmd.clone, body=%wide.region_2.4_spmd.clone.sunk | while | flops 476 | bytes 331 | solution.py:52
  136.4 22.9 %all-gather.6.cloned.1.call-done = bf16[128,8192]{1,0:T(8,128)(2,1)} async-done(((bf16[32,8192]{1,0:T(8,128)(2,1)}), bf16[128,8192]{1,0:T(8,128)(2,1)}) %all-gather.6.cloned.1.call-update) | async-done | bytes 2097168 | tf_op jit(solution)/shard_map/all_gather | solution.py:90
  160.9 116.4 %while.32 = (s32[]{:T(128)}, bf16[32,8192]{1,0:T(8,128)(2,1)S(1)}, bf16[4,32,8192]{2,1,0:T(8,128)(2,1)}, bf16[4,32,128]{2,1,0:T(8,128)(2,1)S(1)}, bf16[4,32,128]...) while((s32[]{:T(128)}, bf16[32,8192]{1,0:T(8,128)(2,1)S(1)}, ...), condition=%wide.region_6.7_spmd, body=%wide.region_5.6_spmd.sunk | while | flops 202702848 | bytes 22661404 | solution.py:113
  162.0 1.7 bitcast_dynamic-update-slice_fusion.6
  163.6 2.1 bitcast_dynamic-update-slice_fusion.7
  169.1 2.7 collective-permute-done
  172.9 1.7 bitcast_dynamic-update-slice_fusion.6
  174.6 2.1 bitcast_dynamic-update-slice_fusion.7
  180.0 9.1 %collective-permute-done = bf16[32,8192]{1,0:T(8,128)(2,1)S(1)} collective-permute-done((bf16[32,8192]{1,0:T(8,128)(2,1)}, bf16[32,8192]{1,0:T(8,128)(2,1)S(1)}, u32[]{:S(2)}, u32[]{:S(2)}) %collective-permute-start) | collective-permute-done | bytes 524320 | tf_op jit(solution)/shard_map/while/body/eval_jaxpr/ppermute | solution.py:17
  190.3 1.7 bitcast_dynamic-update-slice_fusion.6
  191.9 2.1 bitcast_dynamic-update-slice_fusion.7
  194.5 1.6 fusion.54
  197.4 9.4 %collective-permute-done = bf16[32,8192]{1,0:T(8,128)(2,1)S(1)} collective-permute-done((bf16[32,8192]{1,0:T(8,128)(2,1)}, bf16[32,8192]{1,0:T(8,128)(2,1)S(1)}, u32[]{:S(2)}, u32[]{:S(2)}) %collective-permute-start) | collective-permute-done | bytes 524320 | tf_op jit(solution)/shard_map/while/body/eval_jaxpr/ppermute | solution.py:17
  207.9 1.7 bitcast_dynamic-update-slice_fusion.6
  209.6 2.1 bitcast_dynamic-update-slice_fusion.7
  215.0 9.4 %collective-permute-done = bf16[32,8192]{1,0:T(8,128)(2,1)S(1)} collective-permute-done((bf16[32,8192]{1,0:T(8,128)(2,1)}, bf16[32,8192]{1,0:T(8,128)(2,1)S(1)}, u32[]{:S(2)}, u32[]{:S(2)}) %collective-permute-start) | collective-permute-done | bytes 524320 | tf_op jit(solution)/shard_map/while/body/eval_jaxpr/ppermute | solution.py:17
  225.5 1.7 bitcast_dynamic-update-slice_fusion.6
  227.2 2.1 bitcast_dynamic-update-slice_fusion.7
  229.7 1.6 fusion.54
  232.6 9.4 %collective-permute-done = bf16[32,8192]{1,0:T(8,128)(2,1)S(1)} collective-permute-done((bf16[32,8192]{1,0:T(8,128)(2,1)}, bf16[32,8192]{1,0:T(8,128)(2,1)S(1)}, u32[]{:S(2)}, u32[]{:S(2)}) %collective-permute-start) | collective-permute-done | bytes 524320 | tf_op jit(solution)/shard_map/while/body/eval_jaxpr/ppermute | solution.py:17
  243.2 1.7 bitcast_dynamic-update-slice_fusion.6
  244.8 2.1 bitcast_dynamic-update-slice_fusion.7
  250.3 9.4 %collective-permute-done = bf16[32,8192]{1,0:T(8,128)(2,1)S(1)} collective-permute-done((bf16[32,8192]{1,0:T(8,128)(2,1)}, bf16[32,8192]{1,0:T(8,128)(2,1)S(1)}, u32[]{:S(2)}, u32[]{:S(2)}) %collective-permute-start) | collective-permute-done | bytes 524320 | tf_op jit(solution)/shard_map/while/body/eval_jaxpr/ppermute | solution.py:17
  260.8 1.7 bitcast_dynamic-update-slice_fusion.6
  262.4 2.0 bitcast_dynamic-update-slice_fusion.7
  267.9 9.4 %collective-permute-done = bf16[32,8192]{1,0:T(8,128)(2,1)S(1)} collective-permute-done((bf16[32,8192]{1,0:T(8,128)(2,1)}, bf16[32,8192]{1,0:T(8,128)(2,1)S(1)}, u32[]{:S(2)}, u32[]{:S(2)}) %collective-permute-start) | collective-permute-done | bytes 524320 | tf_op jit(solution)/shard_map/while/body/eval_jaxpr/ppermute | solution.py:17
  277.3 2.5 fusion.16
  280.5 2.4 pad_maximum_fusion
  282.9 95.5 %reduce-scatter.2.cloned.1.call-done = bf16[1024,256]{0,1:T(8,128)(2,1)} async-done(((bf16[8192,256]{0,1:T(8,128)(2,1)}), bf16[1024,256]{0,1:T(8,128)(2,1)}) %reduce-scatter.2.cloned.1.call-update) | async-done | bytes 524304 | tf_op jit(solution)/shard_map/reduce_scatter | solution.py:119
  (123 shorter events, 66.6 us)
Async XLA Ops:
  7.2 55.0 %copy-start = (bf16[1,32,8192]{2,1,0:T(8,128)(2,1)S(1)}, bf16[1,32,8192]{2,1,0:T(8,128)(2,1)}, u32[]{:S(2)}) copy-start(bf16[1,32,8192]{2,1,0:T(8,128)(2,1)} %param.14) | copy-start | bytes 1572868
  7.2 55.0 %all-gather.4.cloned.1.call-start = ((), (), s32[]{:S(2)}) async-start(), calls=%async_computation.1 | async-start | bytes 2359296 | tf_op jit(solution)/shard_map/all_gather | solution.py:67
  7.9 151.4 %all-gather.6.cloned.1.call-start = ((), (), s32[]{:S(2)}) async-start(), calls=%async_computation.3 | async-start | bytes 2621440 | tf_op jit(solution)/shard_map/all_gather | solution.py:90
  62.2 2.2 copy-start.3
  134.5 26.3 %copy-start.5 = (f32[6]{0:T(128)}, f32[6]{0:T(128)S(1)}, u32[]{:S(2)}) copy-start(f32[6]{0:T(128)S(1)} %get-tuple-element.286) | copy-start | bytes 76
  136.3 24.6 %copy-start.1 = (bf16[1,8192,128]{2,1,0:T(8,128)(2,1)S(1)}, bf16[1,8192,128]{2,1,0:T(8,128)(2,1)}, u32[]{:S(2)}) copy-start(bf16[1,8192,128]{2,1,0:T(8,128)(2,1)} %param.12) | copy-start | bytes 6291460
  136.3 242.1 %reduce-scatter.2.cloned.1.call-start = ((), (), s32[]{:S(2)}) async-start(), calls=%async_computation.2 | async-start | bytes 4718592 | tf_op jit(solution)/shard_map/reduce_scatter | solution.py:119
  162.0 3.7 copy-start.2
  167.8 4.0 %collective-permute-start = (bf16[32,8192]{1,0:T(8,128)(2,1)}, bf16[32,8192]{1,0:T(8,128)(2,1)S(1)}, u32[]{:S(2)}, u32[]{:S(2)}) collective-permute-start(bf16[32,8192]{1,0:T(8,128)(2,1)} %fusion.54), channel_id=1, source_target_pairs={{8,0},{16,8},{24,16},{9,1},{17,9},{25,17},{10,2},{18,10},{26,18},{... | collective-permute-start | bytes 1572872 | tf_op jit(solution)/shard_map/while/body/eval_jaxpr/ppermute | solution.py:17
  172.9 3.7 copy-start.2
  178.7 10.4 %collective-permute-start = (bf16[32,8192]{1,0:T(8,128)(2,1)}, bf16[32,8192]{1,0:T(8,128)(2,1)S(1)}, u32[]{:S(2)}, u32[]{:S(2)}) collective-permute-start(bf16[32,8192]{1,0:T(8,128)(2,1)} %fusion.54), channel_id=1, source_target_pairs={{8,0},{16,8},{24,16},{9,1},{17,9},{25,17},{10,2},{18,10},{26,18},{... | collective-permute-start | bytes 1572872 | tf_op jit(solution)/shard_map/while/body/eval_jaxpr/ppermute | solution.py:17
  190.3 3.7 copy-start.2
  196.1 10.7 %collective-permute-start = (bf16[32,8192]{1,0:T(8,128)(2,1)}, bf16[32,8192]{1,0:T(8,128)(2,1)S(1)}, u32[]{:S(2)}, u32[]{:S(2)}) collective-permute-start(bf16[32,8192]{1,0:T(8,128)(2,1)} %fusion.54), channel_id=1, source_target_pairs={{8,0},{16,8},{24,16},{9,1},{17,9},{25,17},{10,2},{18,10},{26,18},{... | collective-permute-start | bytes 1572872 | tf_op jit(solution)/shard_map/while/body/eval_jaxpr/ppermute | solution.py:17
  207.9 3.7 copy-start.2
  213.7 10.7 %collective-permute-start = (bf16[32,8192]{1,0:T(8,128)(2,1)}, bf16[32,8192]{1,0:T(8,128)(2,1)S(1)}, u32[]{:S(2)}, u32[]{:S(2)}) collective-permute-start(bf16[32,8192]{1,0:T(8,128)(2,1)} %fusion.54), channel_id=1, source_target_pairs={{8,0},{16,8},{24,16},{9,1},{17,9},{25,17},{10,2},{18,10},{26,18},{... | collective-permute-start | bytes 1572872 | tf_op jit(solution)/shard_map/while/body/eval_jaxpr/ppermute | solution.py:17
  225.5 3.7 copy-start.2
  231.3 10.7 %collective-permute-start = (bf16[32,8192]{1,0:T(8,128)(2,1)}, bf16[32,8192]{1,0:T(8,128)(2,1)S(1)}, u32[]{:S(2)}, u32[]{:S(2)}) collective-permute-start(bf16[32,8192]{1,0:T(8,128)(2,1)} %fusion.54), channel_id=1, source_target_pairs={{8,0},{16,8},{24,16},{9,1},{17,9},{25,17},{10,2},{18,10},{26,18},{... | collective-permute-start | bytes 1572872 | tf_op jit(solution)/shard_map/while/body/eval_jaxpr/ppermute | solution.py:17
  243.1 3.8 copy-start.2
  249.0 10.7 %collective-permute-start = (bf16[32,8192]{1,0:T(8,128)(2,1)}, bf16[32,8192]{1,0:T(8,128)(2,1)S(1)}, u32[]{:S(2)}, u32[]{:S(2)}) collective-permute-start(bf16[32,8192]{1,0:T(8,128)(2,1)} %fusion.54), channel_id=1, source_target_pairs={{8,0},{16,8},{24,16},{9,1},{17,9},{25,17},{10,2},{18,10},{26,18},{... | collective-permute-start | bytes 1572872 | tf_op jit(solution)/shard_map/while/body/eval_jaxpr/ppermute | solution.py:17
  260.8 3.7 copy-start.2
  266.6 10.7 %collective-permute-start = (bf16[32,8192]{1,0:T(8,128)(2,1)}, bf16[32,8192]{1,0:T(8,128)(2,1)S(1)}, u32[]{:S(2)}, u32[]{:S(2)}) collective-permute-start(bf16[32,8192]{1,0:T(8,128)(2,1)} %fusion.54), channel_id=1, source_target_pairs={{8,0},{16,8},{24,16},{9,1},{17,9},{25,17},{10,2},{18,10},{26,18},{... | collective-permute-start | bytes 1572872 | tf_op jit(solution)/shard_map/while/body/eval_jaxpr/ppermute | solution.py:17
  277.3 2.5 copy-start.4
Sparse Core Ops, SparseCore 0:
  10.1 51.9 all-gather.3
  136.4 22.7 all-gather.5
  283.0 95.2 reduce-scatter.1
where the time goes:
time: 389 us; the launch traced here: 388 us
  waiting for transfers between devices  231 us (59%)
  matrix products  49.5 us (13%)
  blocking collectives  39.3 us (10%)
  other arithmetic  31.6 us (8%)
  between operations  14.5 us (4%)
  local copies, waits for them, and re-layouts  12.1 us (3%)
  starting transfers between devices  9.08 us (2%)
    reduce_scatter x1, waiting for transfers between devices, body(): lax.psum_scatter(jnp.concatenate([part_down, part_up], axis=1).astype(jnp...  95.5 us
    ppermute x7, waiting for transfers between devices, from_behind(): lax.ppermute(value, axis, [(source, source + steps) for source in range(f...  58.9 us
    all_gather x1, waiting for transfers between devices, body(): weights = lax.all_gather(head_weights, 'dp', axis=0, tiled=True)  53.4 us
    psum x1, blocking collectives, body(): gram_matrix = lax.psum(partial_gram, ('section', 'dp'))  39.3 us
    all_gather x1, waiting for transfers between devices, body(): cotangents = lax.all_gather(own_grad[None], 'section', axis=0, tiled=True)  22.9 us
    dot_general x20, matrix products, advance(): jnp.dot(gram_matrix, weights, precision=lax.Precision.HIGHEST) / trace_sum  15 us
    dynamic_update_slice x7, other arithmetic, store_row(): return lax.dynamic_update_index_in_dim(buffer, chosen, index, 0)  14.5 us
    div x20, other arithmetic, advance(): return weights / jnp.sum(weights)  13 us
  transfers between devices with their start and end apart: 10, of which 10 were waited for; matrix products, arithmetic and copies ran while one was open for 0% of the time, Pallas kernels for 0%

commit v1 on v0

v1 whole, which is shorter than its diff:
```python
import functools

import jax
import jax.numpy as jnp
from jax import lax
from jax.experimental import pallas as pl
from jax.experimental.pallas import tpu as pltpu
from jax.sharding import PartitionSpec as P

TASKS = 6
STEPS = 20
STEP_RATE = 3.0
TASK_ROWS = 8

REP, XIN, PRED, KSUM, KALL, GRAM, INNER, TSUM, TALL = range(9)
DOWN, RESID, CHAIN = range(3)

F32 = jnp.float32
BF16 = jnp.bfloat16


def round_up(value, unit):
    return -(-value // unit) * unit


def mm(a, b, precision=None):
    return jnp.dot(a, b, preferred_element_type=F32, precision=precision)


def mm_t(a, b):
    return lax.dot_general(a, b, (((0,), (0,)), ((), ())), preferred_element_type=F32)


def kernel(
    sections, peers, heads,
    x_hbm, down_hbm, up_hbm, rep_hbm, w_hbm, targets, head_task,
    down_out, up_out, mix_out,
    x_buf, down_buf, up_buf, basis, repg, xg, pred, predg, kpart, kslots, kall,
    resid, gpart, gslots, inner, innerg, tpart, tslots, tsum, active, slope, branch,
    local_sem, dp_send, dp_recv, sec_send, sec_recv,
):
    rows, width = x_buf.shape
    rank = down_buf.shape[1]
    block = width // peers
    toks = repg.shape[1]
    krows = kslots.shape[1]
    trows = tslots.shape[1]
    me = lax.axis_index("dp")
    sec = lax.axis_index("section")

    def columns(index):
        return pl.ds(pl.multiple_of(index * block, block), block)

    def blocks(index):
        return pl.ds(pl.multiple_of(index * block, block), block)

    def dp_copy(ex, src, dst, slot, peer):
        return pltpu.make_async_remote_copy(
            src_ref=src, dst_ref=dst, send_sem=dp_send.at[ex, peer], recv_sem=dp_recv.at[ex, slot],
            device_id={"dp": peer}, device_id_type=pl.DeviceIdType.MESH,
        )

    def sec_copy(ex, src, dst, slot, peer):
        return pltpu.make_async_remote_copy(
            src_ref=src, dst_ref=dst, send_sem=sec_send.at[ex, peer], recv_sem=sec_recv.at[ex, slot],
            device_id={"section": peer}, device_id_type=pl.DeviceIdType.MESH,
        )

    def each_dp(action):
        @pl.loop(1, peers)
        def _(k):
            action(lax.rem(me + k, peers))

    def each_sec(action):
        @pl.loop(1, sections)
        def _(k):
            action(lax.rem(sec + k, sections))

    def dp_start(ex, src_of, dst):
        each_dp(lambda peer: dp_copy(ex, src_of(peer), dst, me, peer).start())

    def dp_wait(ex, dst_of):
        each_dp(lambda peer: dp_copy(ex, dst_of(peer), dst_of(peer), peer, peer).wait_recv())

    def dp_sent(ex, src_of):
        each_dp(lambda peer: dp_copy(ex, src_of(peer), src_of(peer), peer, peer).wait_send())

    def sec_start(ex, src, dst):
        each_sec(lambda peer: sec_copy(ex, src, dst, sec, peer).start())

    def sec_wait(ex, dst_of):
        each_sec(lambda peer: sec_copy(ex, dst_of(peer), dst_of(peer), peer, peer).wait_recv())

    def sec_sent(ex, src):
        each_sec(lambda peer: sec_copy(ex, src, src, peer, peer).wait_send())

    my_block = blocks(me)
    local = [
        pltpu.make_async_copy(rep_hbm.at[:, columns(me)], repg.at[me], local_sem.at[0]),
        pltpu.make_async_copy(w_hbm, basis.at[sec], local_sem.at[1]),
        pltpu.make_async_copy(x_hbm, x_buf, local_sem.at[2]),
        pltpu.make_async_copy(down_hbm, down_buf, local_sem.at[3]),
        pltpu.make_async_copy(up_hbm.at[my_block], up_buf, local_sem.at[4]),
        pltpu.make_async_copy(x_hbm.at[:, columns(me)], xg.at[me], local_sem.at[5]),
    ]
    for copy in local:
        copy.start()

    barrier = pltpu.get_barrier_semaphore()
    each_dp(lambda peer: pl.semaphore_signal(
        barrier, inc=1, device_id={"dp": peer}, device_id_type=pl.DeviceIdType.MESH))
    each_sec(lambda peer: pl.semaphore_signal(
        barrier, inc=1, device_id={"section": peer}, device_id_type=pl.DeviceIdType.MESH))
    pl.semaphore_wait(barrier, peers + sections - 2)

    dp_start(REP, lambda peer: rep_hbm.at[:, columns(peer)], repg.at[me])
    sec_start(DOWN, down_hbm.at[my_block], basis.at[sec])
    dp_start(XIN, lambda peer: x_hbm.at[:, columns(peer)], xg.at[me])

    local[2].wait()
    local[3].wait()

    def add_preact(k, total):
        return total + mm(x_buf[:, columns(k)], down_buf[blocks(k), :])

    preact = lax.fori_loop(0, peers, add_preact, jnp.zeros((rows, rank), F32))
    logistic = jax.nn.sigmoid(preact)
    active[...] = (preact * logistic).astype(BF16)
    slope[...] = logistic * (1.0 + preact * (1.0 - logistic))

    local[0].wait()
    local[1].wait()
    dp_wait(REP, lambda peer: repg.at[peer])
    head_block = basis[sec]

    @pl.loop(0, peers)
    def _(n):
        pred[n] = mm(repg[n], head_block)

    dp_start(PRED, lambda peer: pred.at[peer], predg.at[me])
    predg[me] = pred[me]

    local[4].wait()
    sec_wait(DOWN, lambda peer: basis.at[peer])
    used = (sections + 1) * rank
    if kpart.shape[0] > used:
        kpart[used:, :] = jnp.zeros((kpart.shape[0] - used, rank), F32)
    up_block = up_buf[...]
    for j in range(sections):
        kpart[j * rank : (j + 1) * rank, :] = mm_t(basis[j], up_block)
    kpart[sections * rank : used, :] = mm_t(head_block, head_block)

    def kspan(index):
        return pl.ds(pl.multiple_of(index * krows, 8), krows)

    dp_start(KSUM, lambda peer: kpart.at[kspan(peer)], kslots.at[me])
    kslots[me] = kpart[kspan(me), :]

    dp_wait(PRED, lambda peer: predg.at[peer])
    predicted = lax.fori_loop(1, peers, lambda n, total: total + predg[n], predg[0])
    resid[sec] = (predicted - targets[...].astype(F32)).astype(BF16)
    sec_start(RESID, resid.at[sec], resid.at[sec])

    dp_wait(KSUM, lambda peer: kslots.at[peer])
    kall[kspan(me), :] = lax.fori_loop(1, peers, lambda n, total: total + kslots[n], kslots[0])
    dp_start(KALL, lambda peer: kall.at[kspan(me)], kall.at[kspan(me)])

    lanes = lax.broadcasted_iota(jnp.int32, (heads, rank), 1)
    owner = lax.broadcasted_iota(jnp.int32, (heads, rank), 0) * (rank // heads)
    of_head = (lanes >= owner) & (lanes < owner + rank // heads)
    column_task = jnp.sum(
        jnp.where(of_head, head_task[...].astype(F32), 0.0), axis=0, keepdims=True
    )
    wide = lax.broadcasted_iota(jnp.int32, (rank, rank), 0).astype(F32)
    task_wide = (wide == column_task).astype(F32)
    task_tall = task_wide[:TASK_ROWS]

    sec_wait(RESID, lambda peer: resid.at[peer])
    tokens = resid[...].reshape(rows, rank)
    outer = mm_t(tokens, tokens)
    dp_wait(KALL, lambda peer: kall.at[kspan(peer)])
    product = outer * kall[sections * rank : used, :]
    half = mm(task_tall, product, lax.Precision.HIGHEST)
    share = lax.dot_general(
        half, task_wide, (((1,), (1,)), ((), ())),
        preferred_element_type=F32, precision=lax.Precision.HIGHEST,
    )
    gpart[...] = share
    gslots[me] = share
    dp_start(GRAM, lambda peer: gpart, gslots.at[me])
    dp_wait(GRAM, lambda peer: gslots.at[peer])
    gram = lax.fori_loop(1, peers, lambda n, total: total + gslots[n], gslots[0])

    down_index = lax.broadcasted_iota(jnp.int32, gram.shape, 0)
    lane_index = lax.broadcasted_iota(jnp.int32, gram.shape, 1)
    trace = jnp.sum(
        jnp.sum(jnp.where(down_index == lane_index, gram, 0.0), axis=1, keepdims=True),
        axis=0, keepdims=True,
    ) + 1e-6
    scaled = gram * (-STEP_RATE / trace)
    tall = jnp.where(down_index[:, :1] < TASKS, 1.0 / TASKS, 0.0).astype(F32)
    flat = jnp.where(lane_index[:1] < TASKS, 1.0 / TASKS, 0.0).astype(F32)
    for _ in range(STEPS):
        along = jnp.sum(scaled * tall, axis=0, keepdims=True)
        across = jnp.sum(scaled * flat, axis=1, keepdims=True)
        tall = tall * jnp.exp(across)
        flat = flat * jnp.exp(along)
        inverse = 1.0 / jnp.sum(tall, axis=0, keepdims=True)
        tall = tall * inverse
        flat = flat * inverse
    mix_out[...] = jnp.broadcast_to(flat, mix_out.shape)

    column_weight = jnp.sum(task_tall * tall, axis=0, keepdims=True)
    weighted = (tokens.astype(F32) * column_weight).astype(BF16)

    def kmat(index):
        return kall[pl.ds(pl.multiple_of(index * rank, rank), rank), :].astype(BF16)

    def tspan(index):
        return pl.ds(pl.multiple_of(index * trows, 16), trows)

    def tmat(index):
        return pl.ds(pl.multiple_of(index * rank, rank), rank)

    tpart[...] = jnp.zeros(tpart.shape, BF16)
    tpart[tmat(sec), :] = mm_t(weighted, active[...]).astype(BF16)
    branch[...] = mm(weighted, kmat(sec))
    for j in range(sections - 1, -1, -1):
        @pl.when(sec == j)
        def _():
            inner[j] = (branch[...] * slope[...]).astype(BF16)
            for lower in range(j):
                sec_copy(CHAIN, inner.at[j], inner.at[j], j, lower).start()

        @pl.when(sec < j)
        def _():
            sec_copy(CHAIN, inner.at[j], inner.at[j], j, j).wait_recv()
            branch[...] += mm(inner[j], kmat(j))
            tpart[j * rank : (j + 1) * rank, :] = mm_t(inner[j], active[...]).astype(BF16)

    dp_start(TSUM, lambda peer: tpart.at[tspan(peer)], tslots.at[me])
    dp_start(INNER, lambda peer: inner.at[sec], innerg.at[me])
    tslots[me] = tpart[tspan(me), :]
    innerg[me] = inner[sec]

    dp_wait(TSUM, lambda peer: tslots.at[peer])
    tsum[tspan(me), :] = lax.fori_loop(
        1, peers, lambda n, total: total + tslots[n].astype(F32), tslots[0].astype(F32)
    ).astype(BF16)
    dp_start(TALL, lambda peer: tsum.at[tspan(me)], tsum.at[tspan(me)])

    local[5].wait()
    dp_wait(INNER, lambda peer: innerg.at[peer])
    dp_wait(XIN, lambda peer: xg.at[peer])
    down_out[...] = jnp.zeros(down_out.shape, F32)

    @pl.loop(0, peers)
    def _(n):
        down_out[...] += mm_t(xg[n], innerg[n])

    dp_wait(TALL, lambda peer: tsum.at[tspan(peer)])
    up_out[...] = mm(basis[0], tsum[:rank, :])

    @pl.loop(1, sections)
    def _(n):
        up_out[...] += mm(basis[n], tsum[tmat(n), :])

    dp_sent(REP, lambda peer: repg.at[me])
    dp_sent(XIN, lambda peer: xg.at[me])
    dp_sent(PRED, lambda peer: pred.at[peer])
    dp_sent(KSUM, lambda peer: kpart.at[kspan(peer)])
    dp_sent(KALL, lambda peer: kall.at[kspan(me)])
    dp_sent(GRAM, lambda peer: gpart)
    dp_sent(INNER, lambda peer: inner.at[sec])
    dp_sent(TSUM, lambda peer: tpart.at[tspan(peer)])
    dp_sent(TALL, lambda peer: tsum.at[tspan(me)])
    sec_sent(DOWN, basis.at[sec])
    sec_sent(RESID, resid.at[sec])
    for j in range(1, sections):
        @pl.when(sec == j)
        def _():
            for lower in range(j):
                sec_copy(CHAIN, inner.at[j], inner.at[j], lower, lower).wait_send()


def body(
    section_inputs, adapter_down, adapter_up, representation, head_weights, head_targets, head_task
):
    sections = lax.axis_size("section")
    peers = lax.axis_size("dp")
    _, micro, toks, width = section_inputs.shape
    rank = adapter_down.shape[2]
    rows = micro * toks
    block = width // peers
    krows = round_up(-(-(sections + 1) * rank // peers), 16)
    trows = round_up(-(-sections * rank // peers), 16)
    vmem = pl.BlockSpec(memory_space=pltpu.VMEM)
    hbm = pl.BlockSpec(memory_space=pl.ANY)
    scratch = [
        pltpu.VMEM((rows, width), BF16),
        pltpu.VMEM((width, rank), BF16),
        pltpu.VMEM((block, rank), BF16),
        pltpu.VMEM((sections, block, rank), BF16),
        pltpu.VMEM((peers, toks, block), BF16),
        pltpu.VMEM((peers, rows, block), BF16),
        pltpu.VMEM((peers, toks, rank), F32),
        pltpu.VMEM((peers, toks, rank), F32),
        pltpu.VMEM((peers * krows, rank), F32),
        pltpu.VMEM((peers, krows, rank), F32),
        pltpu.VMEM((peers * krows, rank), F32),
        pltpu.VMEM((sections, toks, rank), BF16),
        pltpu.VMEM((TASK_ROWS, rank), F32),
        pltpu.VMEM((peers, TASK_ROWS, rank), F32),
        pltpu.VMEM((sections, rows, rank), BF16),
        pltpu.VMEM((peers, rows, rank), BF16),
        pltpu.VMEM((peers * trows, rank), BF16),
        pltpu.VMEM((peers, trows, rank), BF16),
        pltpu.VMEM((peers * trows, rank), BF16),
        pltpu.VMEM((rows, rank), BF16),
        pltpu.VMEM((rows, rank), F32),
        pltpu.VMEM((rows, rank), F32),
        pltpu.SemaphoreType.DMA((6,)),
        pltpu.SemaphoreType.DMA((9, peers)),
        pltpu.SemaphoreType.DMA((9, peers)),
        pltpu.SemaphoreType.DMA((3, sections)),
        pltpu.SemaphoreType.DMA((3, sections)),
    ]
    down, up, mix = pl.pallas_call(
        functools.partial(kernel, sections, peers, head_task.shape[0]),
        out_shape=(
            jax.ShapeDtypeStruct((block, rank), F32),
            jax.ShapeDtypeStruct((block, rank), F32),
            jax.ShapeDtypeStruct((TASK_ROWS, rank), F32),
        ),
        in_specs=[hbm] * 5 + [vmem] * 2,
        out_specs=(vmem, vmem, vmem),
        scratch_shapes=scratch,
        compiler_params=pltpu.CompilerParams(
            collective_id=0, has_side_effects=True, vmem_limit_bytes=48 << 20
        ),
    )(
        section_inputs.reshape(rows, width), adapter_down[0], adapter_up[0], representation[0],
        head_weights, head_targets[0], head_task,
    )
    return (down[None], up[None], mix[0, :TASKS])


def solution(mesh):
    in_specs = (
        P("section", None, "dp", None),
        P("section", None, None),
        P("section", None, None),
        P("section", "dp", None),
        P("dp", None),
        P("section", "dp", None),
        P(),
    )
    out_specs = (P("section", "dp", None), P("section", "dp", None), P())
    return jax.shard_map(body, mesh=mesh, in_specs=in_specs, out_specs=out_specs, check_vma=False)
```

time: 389 us -> 119 us (0.31)
  waiting for transfers between devices: 231 us -> 0 us
  Pallas kernels: 0 us -> 109 us
  matrix products: 49.5 us -> 0 us
  blocking collectives: 39.3 us -> 0 us
  other arithmetic: 31.6 us -> 0 us
  between operations: 14.5 us -> 0.64 us
  starting transfers between devices: 9.08 us -> 0 us
    pallas_call x0 -> x1, Pallas kernels: none -> 109 us  [body(): pl.pallas_call(functools.partial(kernel, sections, peers, head_task.shape...]
    reduce_scatter x1 -> x0, waiting for transfers between devices: 95.5 us -> none  [body(): lax.psum_scatter(jnp.concatenate([part_down, part_up], axis=1).astype(jnp...]
    all_gather x2 -> x0, waiting for transfers between devices: 76.3 us -> none  [the longest x1 53.4 us: body(): weights = lax.all_gather(head_weights, 'dp', axis=0, tiled=True)]
    ppermute x7 -> x0, waiting for transfers between devices: 58.9 us -> none  [from_behind(): lax.ppermute(value, axis, [(source, source + steps) for source in range(f...]
    dot_general x49 -> x0, matrix products: 49.5 us -> none  [the longest x20 15 us: advance(): jnp.dot(gram_matrix, weights, precision=lax.Precision.HIGHEST) / trace_sum]
    psum x1 -> x0, blocking collectives: 39.3 us -> none  [body(): gram_matrix = lax.psum(partial_gram, ('section', 'dp'))]
    dynamic_update_slice x7 -> x0, other arithmetic: 14.5 us -> none  [store_row(): return lax.dynamic_update_index_in_dim(buffer, chosen, index, 0)]
    div x20 -> x0, other arithmetic: 13 us -> none  [advance(): return weights / jnp.sum(weights)]
  transfers between devices with their start and end apart: 10 -> 0, of which waited for: 10 -> 0; matrix products, arithmetic and copies ran while one was open for 0% -> 0% of each run, Pallas kernels for 0% -> 0%
where the time goes in v1:
time: 119 us
  Pallas kernels  109 us (92%)
  local copies, waits for them, and re-layouts  8.7 us (7%)
    pallas_call x1, Pallas kernels, body(): pl.pallas_call(functools.partial(kernel, sections, peers, head_task.shape...  109 us
    unnamed x13, local copies, waits for them, and re-layouts  8.18 us

profile of v1, /device:TPU:0, one launch (start us, length us, event | category | flops | bytes accessed | tf_op | source)
XLA Modules:
  0.0 118.5 jit_solution(15768849480293910175)
XLA Ops:
  0.6 0.7 copy.10.head_task
  1.4 0.0 copy-start
  1.4 1.6 %copy-done = bf16[1,4,32,8192]{3,2,1,0:T(8,128)(2,1)S(1)} copy-done((bf16[1,4,32,8192]{3,2,1,0:T(8,128)(2,1)S(1)}, bf16[1,4,32,8192]{3,2,1,0:T(8,128)(2,1)}, u32[]{:S(2)}) %copy-start) | copy-done | bytes 2097176
  3.0 0.0 copy-start.1
  3.0 1.6 %copy-done.1 = bf16[1,8192,128]{2,1,0:T(8,128)(2,1)S(1)} copy-done((bf16[1,8192,128]{2,1,0:T(8,128)(2,1)S(1)}, bf16[1,8192,128]{2,1,0:T(8,128)(2,1)}, u32[]{:S(2)}) %copy-start.1) | copy-done | bytes 2097176
  4.5 0.0 copy-start.2
  4.5 1.0 copy-done.2
  5.6 0.0 copy-start.3
  5.6 0.9 copy-done.3
  6.5 0.0 copy-start.4
  6.5 0.7 copy-done.4
  7.2 109.2 %shard_map.94 = (f32[1024,128]{1,0:T(8,128)S(1)}, f32[1024,128]{1,0:T(8,128)S(1)}, f32[8,128]{1,0:T(8,128)S(1)}) custom-call(bf16[128,8192]{1,0:T(8,128)(2,1)S(1)} %bitcast.9, bf16[8192,128]{1,0:T(8,128)(2,1)S(1)} %bitcast.10, bf16[8192,128]{1,0:T(8,128)(2,1)} %bitcast.15, bf16[32,8192]{1,0:T(8,128)(2,1)S(1)} %bitcast.13, bf16[1024,128]{1,0:T(8,128)(2,1)S(1)} %copy-done.3, ...), custom_call_target="tpu_custom_call" | custom-call | tf_op jit(solution)/shard_map/pallas_call | solution.py:328
  116.4 0.5 slice_bitcast_fusion
  116.9 0.8 copy.13
  117.7 0.8 copy.14
Async XLA Ops:
  1.4 1.6 %copy-start = (bf16[1,4,32,8192]{3,2,1,0:T(8,128)(2,1)S(1)}, bf16[1,4,32,8192]{3,2,1,0:T(8,128)(2,1)}, u32[]{:S(2)}) copy-start(bf16[1,4,32,8192]{3,2,1,0:T(8,128)(2,1)} %param.7) | copy-start | bytes 6291460
  3.0 1.6 %copy-start.1 = (bf16[1,8192,128]{2,1,0:T(8,128)(2,1)S(1)}, bf16[1,8192,128]{2,1,0:T(8,128)(2,1)}, u32[]{:S(2)}) copy-start(bf16[1,8192,128]{2,1,0:T(8,128)(2,1)} %param.8) | copy-start | bytes 6291460
  4.5 1.0 copy-start.2
  5.6 0.9 copy-start.3
  6.5 0.7 copy-start.4

commit v2 on v1

--- a/solution.py
+++ b/solution.py
@@ -12,7 +12,8 @@
 STEP_RATE = 3.0
 TASK_ROWS = 8
 
-REP, XIN, PRED, KSUM, KALL, GRAM, INNER, TSUM, TALL = range(9)
+REP, PRED, KSUM, KALL, WSUM, WALL, GRAM, TSUM, TALL = range(9)
+XOWN, XFAR, INNER = range(3)
 DOWN, RESID, CHAIN = range(3)
 
 F32 = jnp.float32
@@ -35,18 +36,23 @@
     sections, peers, heads,
     x_hbm, down_hbm, up_hbm, rep_hbm, w_hbm, targets, head_task,
     down_out, up_out, mix_out,
-    x_buf, down_buf, up_buf, basis, repg, xg, pred, predg, kpart, kslots, kall,
-    resid, gpart, gslots, inner, innerg, tpart, tslots, tsum, active, slope, branch,
-    local_sem, dp_send, dp_recv, sec_send, sec_recv,
+    x_buf, down_buf, up_buf, basis, repg, xg, pred, predg, kpart, kslots, kall, wpart, wslots, wall,
+    resid, gpart, gslots, inner, innerg, tpart, tslots, tsum, active, slope, branch, cross, crossg,
+    local_sem, dp_send, dp_recv, half_send, half_recv, far_send, far_recv, sec_send, sec_recv,
 ):
     rows, width = x_buf.shape
     rank = down_buf.shape[1]
     block = width // peers
     toks = repg.shape[1]
     krows = kslots.shape[1]
+    wrows = wslots.shape[1]
+    half = peers // 2
     trows = tslots.shape[1]
     me = lax.axis_index("dp")
     sec = lax.axis_index("section")
+    first = lax.div(me, half) * half
+    place = me - first
+    far = lax.rem(me + half, peers)
 
     def columns(index):
         return pl.ds(pl.multiple_of(index * block, block), block)
@@ -65,6 +71,29 @@
             src_ref=src, dst_ref=dst, send_sem=sec_send.at[ex, peer], recv_sem=sec_recv.at[ex, slot],
             device_id={"section": peer}, device_id_type=pl.DeviceIdType.MESH,
         )
+
+    def half_copy(ex, src, dst, slot, peer):
+        return pltpu.make_async_remote_copy(
+            src_ref=src, dst_ref=dst, send_sem=half_send.at[ex, peer], recv_sem=half_recv.at[ex, slot],
+            device_id={"dp": first + peer}, device_id_type=pl.DeviceIdType.MESH,
+        )
+
+    def far_copy(part):
+        return pltpu.make_async_remote_copy(
+            src_ref=cross.at[part], dst_ref=crossg.at[part], send_sem=far_send.at[part],
+            recv_sem=far_recv.at[part], device_id={"dp": far}, device_id_type=pl.DeviceIdType.MESH,
+        )
+
+    def each_half(action):
+        @pl.loop(1, half)
+        def _(k):
+            action(lax.rem(place + k, half))
+
+    def send_inputs(k):
+        peer = lax.rem(place + k, half)
+        half_copy(XOWN, x_hbm.at[:, columns(first + peer)], xg.at[0, place], place, peer).start()
+        beyond = lax.rem(first + peer + half, peers)
+        half_copy(XFAR, x_hbm.at[:, columns(beyond)], xg.at[1, place], place, peer).start()
 
     def each_dp(action):
         @pl.loop(1, peers)
@@ -101,7 +130,8 @@
         pltpu.make_async_copy(x_hbm, x_buf, local_sem.at[2]),
         pltpu.make_async_copy(down_hbm, down_buf, local_sem.at[3]),
         pltpu.make_async_copy(up_hbm.at[my_block], up_buf, local_sem.at[4]),
-        pltpu.make_async_copy(x_hbm.at[:, columns(me)], xg.at[me], local_sem.at[5]),
+        pltpu.make_async_copy(x_hbm.at[:, columns(me)], xg.at[0, place], local_sem.at[5]),
+        pltpu.make_async_copy(x_hbm.at[:, columns(far)], xg.at[1, place], local_sem.at[6]),
     ]
     for copy in local:
         copy.start()
@@ -115,7 +145,26 @@
 
     dp_start(REP, lambda peer: rep_hbm.at[:, columns(peer)], repg.at[me])
     sec_start(DOWN, down_hbm.at[my_block], basis.at[sec])
-    dp_start(XIN, lambda peer: x_hbm.at[:, columns(peer)], xg.at[me])
+
+    local[1].wait()
+    head_block = basis[sec]
+    if wpart.shape[0] > rank:
+        wpart[rank:, :] = jnp.zeros((wpart.shape[0] - rank, rank), F32)
+    wpart[:rank, :] = mm_t(head_block, head_block)
+
+    def wspan(index):
+        return pl.ds(pl.multiple_of(index * wrows, 8), wrows)
+
+    dp_start(WSUM, lambda peer: wpart.at[wspan(peer)], wslots.at[me])
+    wslots[me] = wpart[wspan(me), :]
+
+    cuts = [1 + (half - 1) * part // 3 for part in range(4)]
+
+    def send_part(part):
+        for k in range(cuts[part], cuts[part + 1]):
+            send_inputs(k)
+
+    send_part(0)
 
     local[2].wait()
     local[3].wait()
@@ -129,9 +178,7 @@
     slope[...] = logistic * (1.0 + preact * (1.0 - logistic))
 
     local[0].wait()
-    local[1].wait()
     dp_wait(REP, lambda peer: repg.at[peer])
-    head_block = basis[sec]
 
     @pl.loop(0, peers)
     def _(n):
@@ -139,19 +186,22 @@
 
     dp_start(PRED, lambda peer: pred.at[peer], predg.at[me])
     predg[me] = pred[me]
+    dp_wait(WSUM, lambda peer: wslots.at[peer])
+    wall[wspan(me), :] = lax.fori_loop(1, peers, lambda n, total: total + wslots[n], wslots[0])
+    dp_start(WALL, lambda peer: wall.at[wspan(me)], wall.at[wspan(me)])
+    send_part(1)
 
     local[4].wait()
     sec_wait(DOWN, lambda peer: basis.at[peer])
-    used = (sections + 1) * rank
+    used = sections * rank
     if kpart.shape[0] > used:
-        kpart[used:, :] = jnp.zeros((kpart.shape[0] - used, rank), F32)
-    up_block = up_buf[...]
+        kpart[used:, :] = jnp.zeros((kpart.shape[0] - used, rank), BF16)
+    up_block = up_buf[...].T
     for j in range(sections):
-        kpart[j * rank : (j + 1) * rank, :] = mm_t(basis[j], up_block)
-    kpart[sections * rank : used, :] = mm_t(head_block, head_block)
+        kpart[j * rank : (j + 1) * rank, :] = mm(up_block, basis[j]).astype(BF16)
 
     def kspan(index):
-        return pl.ds(pl.multiple_of(index * krows, 8), krows)
+        return pl.ds(pl.multiple_of(index * krows, 16), krows)
 
     dp_start(KSUM, lambda peer: kpart.at[kspan(peer)], kslots.at[me])
     kslots[me] = kpart[kspan(me), :]
@@ -160,9 +210,12 @@
     predicted = lax.fori_loop(1, peers, lambda n, total: total + predg[n], predg[0])
     resid[sec] = (predicted - targets[...].astype(F32)).astype(BF16)
     sec_start(RESID, resid.at[sec], resid.at[sec])
+    send_part(2)
 
     dp_wait(KSUM, lambda peer: kslots.at[peer])
-    kall[kspan(me), :] = lax.fori_loop(1, peers, lambda n, total: total + kslots[n], kslots[0])
+    kall[kspan(me), :] = lax.fori_loop(
+        1, peers, lambda n, total: total + kslots[n].astype(F32), kslots[0].astype(F32)
+    ).astype(BF16)
     dp_start(KALL, lambda peer: kall.at[kspan(me)], kall.at[kspan(me)])
 
     lanes = lax.broadcasted_iota(jnp.int32, (heads, rank), 1)
@@ -178,11 +231,11 @@
     sec_wait(RESID, lambda peer: resid.at[peer])
     tokens = resid[...].reshape(rows, rank)
     outer = mm_t(tokens, tokens)
-    dp_wait(KALL, lambda peer: kall.at[kspan(peer)])
-    product = outer * kall[sections * rank : used, :]
-    half = mm(task_tall, product, lax.Precision.HIGHEST)
+    dp_wait(WALL, lambda peer: wall.at[wspan(peer)])
+    product = outer * wall[:rank, :]
+    picked = mm(task_tall, product, lax.Precision.HIGHEST)
     share = lax.dot_general(
-        half, task_wide, (((1,), (1,)), ((), ())),
+        picked, task_wide, (((1,), (1,)), ((), ())),
         preferred_element_type=F32, precision=lax.Precision.HIGHEST,
     )
     gpart[...] = share
@@ -210,11 +263,18 @@
         flat = flat * inverse
     mix_out[...] = jnp.broadcast_to(flat, mix_out.shape)
 
+    dp_wait(KALL, lambda peer: kall.at[kspan(peer)])
+
     column_weight = jnp.sum(task_tall * tall, axis=0, keepdims=True)
     weighted = (tokens.astype(F32) * column_weight).astype(BF16)
 
     def kmat(index):
-        return kall[pl.ds(pl.multiple_of(index * rank, rank), rank), :].astype(BF16)
+        return kall[pl.ds(pl.multiple_of(index * rank, rank), rank), :]
+
+    def mm_k(a, index):
+        return lax.dot_general(
+            a, kmat(index), (((1,), (1,)), ((), ())), preferred_element_type=F32
+        )
 
     def tspan(index):
         return pl.ds(pl.multiple_of(index * trows, 16), trows)
@@ -224,7 +284,7 @@
 
     tpart[...] = jnp.zeros(tpart.shape, BF16)
     tpart[tmat(sec), :] = mm_t(weighted, active[...]).astype(BF16)
-    branch[...] = mm(weighted, kmat(sec))
+    branch[...] = mm_k(weighted, sec)
     for j in range(sections - 1, -1, -1):
         @pl.when(sec == j)
         def _():
@@ -235,13 +295,13 @@
         @pl.when(sec < j)
         def _():
             sec_copy(CHAIN, inner.at[j], inner.at[j], j, j).wait_recv()
-            branch[...] += mm(inner[j], kmat(j))
+            branch[...] += mm_k(inner[j], j)
             tpart[j * rank : (j + 1) * rank, :] = mm_t(inner[j], active[...]).astype(BF16)
 
     dp_start(TSUM, lambda peer: tpart.at[tspan(peer)], tslots.at[me])
-    dp_start(INNER, lambda peer: inner.at[sec], innerg.at[me])
+    each_half(lambda peer: half_copy(INNER, inner.at[sec], innerg.at[place], place, peer).start())
     tslots[me] = tpart[tspan(me), :]
-    innerg[me] = inner[sec]
+    innerg[place] = inner[sec]
 
     dp_wait(TSUM, lambda peer: tslots.at[peer])
     tsum[tspan(me), :] = lax.fori_loop(
@@ -250,13 +310,16 @@
     dp_start(TALL, lambda peer: tsum.at[tspan(me)], tsum.at[tspan(me)])
 
     local[5].wait()
-    dp_wait(INNER, lambda peer: innerg.at[peer])
-    dp_wait(XIN, lambda peer: xg.at[peer])
-    down_out[...] = jnp.zeros(down_out.shape, F32)
-
-    @pl.loop(0, peers)
-    def _(n):
-        down_out[...] += mm_t(xg[n], innerg[n])
+    local[6].wait()
+    for ex, ref in ((INNER, innerg), (XOWN, xg.at[0]), (XFAR, xg.at[1])):
+        each_half(lambda peer: half_copy(ex, ref.at[peer], ref.at[peer], peer, peer).wait_recv())
+    spread = innerg[...].reshape(half * rows, rank).T
+    parts = cross.shape[0]
+    span = block // parts
+    for part in range(parts):
+        held = xg[1, :, :, part * span : (part + 1) * span].reshape(half * rows, span)
+        cross[part] = mm(spread, held).astype(BF16)
+        far_copy(part).start()
 
     dp_wait(TALL, lambda peer: tsum.at[tspan(peer)])
     up_out[...] = mm(basis[0], tsum[:rank, :])
@@ -265,13 +328,21 @@
     def _(n):
         up_out[...] += mm(basis[n], tsum[tmat(n), :])
 
+    for part in range(parts):
+        held = xg[0, :, :, part * span : (part + 1) * span].reshape(half * rows, span)
+        own = mm(spread, held)
+        far_copy(part).wait()
+        down_out[part * span : (part + 1) * span, :] = (own + crossg[part].astype(F32)).T
+
     dp_sent(REP, lambda peer: repg.at[me])
-    dp_sent(XIN, lambda peer: xg.at[me])
     dp_sent(PRED, lambda peer: pred.at[peer])
     dp_sent(KSUM, lambda peer: kpart.at[kspan(peer)])
     dp_sent(KALL, lambda peer: kall.at[kspan(me)])
     dp_sent(GRAM, lambda peer: gpart)
-    dp_sent(INNER, lambda peer: inner.at[sec])
+    dp_sent(WSUM, lambda peer: wpart.at[wspan(peer)])
+    dp_sent(WALL, lambda peer: wall.at[wspan(me)])
+    for ex, ref in ((INNER, inner.at[sec]), (XOWN, xg.at[0, place]), (XFAR, xg.at[1, place])):
+        each_half(lambda peer: half_copy(ex, ref, ref, peer, peer).wait_send())
     dp_sent(TSUM, lambda peer: tpart.at[tspan(peer)])
     dp_sent(TALL, lambda peer: tsum.at[tspan(me)])
     sec_sent(DOWN, basis.at[sec])
@@ -292,36 +363,48 @@
     rank = adapter_down.shape[2]
     rows = micro * toks
     block = width // peers
-    krows = round_up(-(-(sections + 1) * rank // peers), 16)
+    krows = round_up(-(-sections * rank // peers), 16)
+    wrows = round_up(-(-rank // peers), 8)
+    half = peers // 2
+    parts = max(1, min(4, block // 128))
     trows = round_up(-(-sections * rank // peers), 16)
     vmem = pl.BlockSpec(memory_space=pltpu.VMEM)
-    hbm = pl.BlockSpec(memory_space=pl.ANY)
+    hbm = pl.BlockSpec(memory_space=pltpu.HBM)
     scratch = [
         pltpu.VMEM((rows, width), BF16),
         pltpu.VMEM((width, rank), BF16),
         pltpu.VMEM((block, rank), BF16),
         pltpu.VMEM((sections, block, rank), BF16),
         pltpu.VMEM((peers, toks, block), BF16),
-        pltpu.VMEM((peers, rows, block), BF16),
+        pltpu.VMEM((2, half, rows, block), BF16),
         pltpu.VMEM((peers, toks, rank), F32),
         pltpu.VMEM((peers, toks, rank), F32),
-        pltpu.VMEM((peers * krows, rank), F32),
-        pltpu.VMEM((peers, krows, rank), F32),
-        pltpu.VMEM((peers * krows, rank), F32),
+        pltpu.VMEM((peers * krows, rank), BF16),
+        pltpu.VMEM((peers, krows, rank), BF16),
+        pltpu.VMEM((peers * krows, rank), BF16),
+        pltpu.VMEM((peers * wrows, rank), F32),
+        pltpu.VMEM((peers, wrows, rank), F32),
+        pltpu.VMEM((peers * wrows, rank), F32),
         pltpu.VMEM((sections, toks, rank), BF16),
         pltpu.VMEM((TASK_ROWS, rank), F32),
         pltpu.VMEM((peers, TASK_ROWS, rank), F32),
         pltpu.VMEM((sections, rows, rank), BF16),
-        pltpu.VMEM((peers, rows, rank), BF16),
+        pltpu.VMEM((half, rows, rank), BF16),
         pltpu.VMEM((peers * trows, rank), BF16),
         pltpu.VMEM((peers, trows, rank), BF16),
         pltpu.VMEM((peers * trows, rank), BF16),
         pltpu.VMEM((rows, rank), BF16),
         pltpu.VMEM((rows, rank), F32),
         pltpu.VMEM((rows, rank), F32),
-        pltpu.SemaphoreType.DMA((6,)),
+        pltpu.VMEM((parts, rank, block // parts), BF16),
+        pltpu.VMEM((parts, rank, block // parts), BF16),
+        pltpu.SemaphoreType.DMA((7,)),
         pltpu.SemaphoreType.DMA((9, peers)),
         pltpu.SemaphoreType.DMA((9, peers)),
+        pltpu.SemaphoreType.DMA((3, half)),
+        pltpu.SemaphoreType.DMA((3, half)),
+        pltpu.SemaphoreType.DMA((parts,)),
+        pltpu.SemaphoreType.DMA((parts,)),
         pltpu.SemaphoreType.DMA((3, sections)),
         pltpu.SemaphoreType.DMA((3, sections)),
     ]
@@ -336,7 +419,7 @@
         out_specs=(vmem, vmem, vmem),
         scratch_shapes=scratch,
         compiler_params=pltpu.CompilerParams(
-            collective_id=0, has_side_effects=True, vmem_limit_bytes=48 << 20
+            collective_id=0, has_side_effects=True, vmem_limit_bytes=62 << 20
         ),
     )(
         section_inputs.reshape(rows, width), adapter_down[0], adapter_up[0], representation[0],

time: 119 us -> 90.3 us (0.76)
  Pallas kernels: 109 us -> 83.1 us
  local copies, waits for them, and re-layouts: 8.7 us -> 6.25 us
    pallas_call x1, Pallas kernels: 109 us -> 83.1 us  [body(): pl.pallas_call(functools.partial(kernel, sections, peers, head_task.shape...]
    unnamed x13 -> x3, local copies, waits for them, and re-layouts: 8.18 us -> 5.06 us
where the time goes in v2:
time: 90.3 us; the launch traced here: 90 us
  Pallas kernels  83.1 us (92%)
  local copies, waits for them, and re-layouts  6.25 us (7%)
    pallas_call x1, Pallas kernels, body(): pl.pallas_call(functools.partial(kernel, sections, peers, head_task.shape...  83.1 us
    unnamed x3, local copies, waits for them, and re-layouts  5.06 us

profile of v2, /device:TPU:0, one launch (start us, length us, event | category | flops | bytes accessed | tf_op | source)
XLA Modules:
  0.0 90.0 jit_solution(5956202921632330007)
XLA Ops:
  0.6 1.3 %copy.10.head_task = s32[8,1]{1,0:T(8,128)} copy(s32[8,1]{0,1:T(1,128)} %param.13) | data formatting | bytes 64 | tf_op args[6]
  2.0 83.1 %shard_map.94 = (f32[1024,128]{1,0:T(8,128)}, f32[1024,128]{1,0:T(8,128)}, f32[8,128]{1,0:T(8,128)}) custom-call(bf16[128,8192]{1,0:T(8,128)(2,1)} %bitcast.9, bf16[8192,128]{1,0:T(8,128)(2,1)} %bitcast.10, bf16[8192,128]{1,0:T(8,128)(2,1)} %bitcast.11, bf16[32,8192]{1,0:T(8,128)(2,1)} %bitcast.14, bf16[1024,128]{1,0:T(8,128)(2,1)} %w_hbm.1, ...), custom_call_target="tpu_custom_call" | custom-call | tf_op jit(solution)/shard_map/pallas_call | solution.py:411
  85.1 1.2 %slice_bitcast_fusion = f32[6]{0:T(128)} fusion(f32[8,128]{1,0:T(8,128)} %get-tuple-element.8), kind=kLoop, calls=%fused_computation | loop fusion | bytes 48 | tf_op jit(solution)/shard_map/squeeze | solution.py:428
  86.3 1.9 %copy.13 = f32[1,1024,128]{2,1,0:T(8,128)} copy(f32[1,1024,128]{2,1,0:T(8,128)} %bitcast.13) | data formatting | bytes 1048576
  88.2 1.9 %copy.14 = f32[1,1024,128]{2,1,0:T(8,128)} copy(f32[1,1024,128]{2,1,0:T(8,128)} %bitcast.12) | data formatting | bytes 1048576

commit v3 on v2

--- a/solution.py
+++ b/solution.py
@@ -89,11 +89,14 @@
         def _(k):
             action(lax.rem(place + k, half))
 
-    def send_inputs(k):
-        peer = lax.rem(place + k, half)
-        half_copy(XOWN, x_hbm.at[:, columns(first + peer)], xg.at[0, place], place, peer).start()
-        beyond = lax.rem(first + peer + half, peers)
-        half_copy(XFAR, x_hbm.at[:, columns(beyond)], xg.at[1, place], place, peer).start()
+    def send_inputs(chunk):
+        peer = lax.rem(place + 1 + chunk // 2, half)
+        if chunk % 2 == 0:
+            source = first + peer
+            half_copy(XOWN, x_hbm.at[:, columns(source)], xg.at[0, place], place, peer).start()
+        else:
+            source = lax.rem(first + peer + half, peers)
+            half_copy(XFAR, x_hbm.at[:, columns(source)], xg.at[1, place], place, peer).start()
 
     def each_dp(action):
         @pl.loop(1, peers)
@@ -158,13 +161,12 @@
     dp_start(WSUM, lambda peer: wpart.at[wspan(peer)], wslots.at[me])
     wslots[me] = wpart[wspan(me), :]
 
-    cuts = [1 + (half - 1) * part // 3 for part in range(4)]
+    chunks = 2 * (half - 1)
+    cuts = [chunks * share // 6 for share in (0, 1, 2, 3, 6)]
 
     def send_part(part):
-        for k in range(cuts[part], cuts[part + 1]):
-            send_inputs(k)
-
-    send_part(0)
+        for chunk in range(cuts[part], cuts[part + 1]):
+            send_inputs(chunk)
 
     local[2].wait()
     local[3].wait()
@@ -178,18 +180,20 @@
     slope[...] = logistic * (1.0 + preact * (1.0 - logistic))
 
     local[0].wait()
-    dp_wait(REP, lambda peer: repg.at[peer])
-
-    @pl.loop(0, peers)
-    def _(n):
-        pred[n] = mm(repg[n], head_block)
-
-    dp_start(PRED, lambda peer: pred.at[peer], predg.at[me])
+    pred[me] = mm(repg[me], head_block)
+
+    @pl.loop(1, peers)
+    def _(k):
+        peer = lax.rem(me - k + peers, peers)
+        dp_copy(REP, repg.at[peer], repg.at[peer], peer, peer).wait_recv()
+        pred[peer] = mm(repg[peer], head_block)
+        dp_copy(PRED, pred.at[peer], predg.at[me], me, peer).start()
+
     predg[me] = pred[me]
     dp_wait(WSUM, lambda peer: wslots.at[peer])
     wall[wspan(me), :] = lax.fori_loop(1, peers, lambda n, total: total + wslots[n], wslots[0])
     dp_start(WALL, lambda peer: wall.at[wspan(me)], wall.at[wspan(me)])
-    send_part(1)
+    send_part(0)
 
     local[4].wait()
     sec_wait(DOWN, lambda peer: basis.at[peer])
@@ -210,7 +214,7 @@
     predicted = lax.fori_loop(1, peers, lambda n, total: total + predg[n], predg[0])
     resid[sec] = (predicted - targets[...].astype(F32)).astype(BF16)
     sec_start(RESID, resid.at[sec], resid.at[sec])
-    send_part(2)
+    send_part(1)
 
     dp_wait(KSUM, lambda peer: kslots.at[peer])
     kall[kspan(me), :] = lax.fori_loop(
@@ -241,8 +245,11 @@
     gpart[...] = share
     gslots[me] = share
     dp_start(GRAM, lambda peer: gpart, gslots.at[me])
+    send_part(2)
     dp_wait(GRAM, lambda peer: gslots.at[peer])
     gram = lax.fori_loop(1, peers, lambda n, total: total + gslots[n], gslots[0])
+
+    send_part(3)
 
     down_index = lax.broadcasted_iota(jnp.int32, gram.shape, 0)
     lane_index = lax.broadcasted_iota(jnp.int32, gram.shape, 1)
@@ -298,16 +305,10 @@
             branch[...] += mm_k(inner[j], j)
             tpart[j * rank : (j + 1) * rank, :] = mm_t(inner[j], active[...]).astype(BF16)
 
+    each_half(lambda peer: half_copy(INNER, inner.at[sec], innerg.at[place], place, peer).start())
     dp_start(TSUM, lambda peer: tpart.at[tspan(peer)], tslots.at[me])
-    each_half(lambda peer: half_copy(INNER, inner.at[sec], innerg.at[place], place, peer).start())
     tslots[me] = tpart[tspan(me), :]
     innerg[place] = inner[sec]
-
-    dp_wait(TSUM, lambda peer: tslots.at[peer])
-    tsum[tspan(me), :] = lax.fori_loop(
-        1, peers, lambda n, total: total + tslots[n].astype(F32), tslots[0].astype(F32)
-    ).astype(BF16)
-    dp_start(TALL, lambda peer: tsum.at[tspan(me)], tsum.at[tspan(me)])
 
     local[5].wait()
     local[6].wait()
@@ -320,6 +321,12 @@
         held = xg[1, :, :, part * span : (part + 1) * span].reshape(half * rows, span)
         cross[part] = mm(spread, held).astype(BF16)
         far_copy(part).start()
+        if part == 0:
+            dp_wait(TSUM, lambda peer: tslots.at[peer])
+            tsum[tspan(me), :] = lax.fori_loop(
+                1, peers, lambda n, total: total + tslots[n].astype(F32), tslots[0].astype(F32)
+            ).astype(BF16)
+            dp_start(TALL, lambda peer: tsum.at[tspan(me)], tsum.at[tspan(me)])
 
     dp_wait(TALL, lambda peer: tsum.at[tspan(peer)])
     up_out[...] = mm(basis[0], tsum[:rank, :])

time: 90.3 us -> 88 us (0.975)
  Pallas kernels: 83.1 us -> 80.8 us
    pallas_call x1, Pallas kernels: 83.1 us -> 80.8 us  [body(): pl.pallas_call(functools.partial(kernel, sections, peers, head_task.shape...]
where the time goes in v3:
time: 88 us; the launch traced here: 87.7 us
  Pallas kernels  80.8 us (92%)
  local copies, waits for them, and re-layouts  6.25 us (7%)
    pallas_call x1, Pallas kernels, body(): pl.pallas_call(functools.partial(kernel, sections, peers, head_task.shape...  80.8 us
    unnamed x3, local copies, waits for them, and re-layouts  5.06 us

profile of v3, /device:TPU:0, one launch (start us, length us, event | category | flops | bytes accessed | tf_op | source)
XLA Modules:
  0.0 87.7 jit_solution(3007690259947655389)
XLA Ops:
  0.6 1.3 %copy.10.head_task = s32[8,1]{1,0:T(8,128)} copy(s32[8,1]{0,1:T(1,128)} %param.13) | data formatting | bytes 64 | tf_op args[6]
  2.0 80.8 %shard_map.94 = (f32[1024,128]{1,0:T(8,128)}, f32[1024,128]{1,0:T(8,128)}, f32[8,128]{1,0:T(8,128)}) custom-call(bf16[128,8192]{1,0:T(8,128)(2,1)} %bitcast.9, bf16[8192,128]{1,0:T(8,128)(2,1)} %bitcast.10, bf16[8192,128]{1,0:T(8,128)(2,1)} %bitcast.11, bf16[32,8192]{1,0:T(8,128)(2,1)} %bitcast.14, bf16[1024,128]{1,0:T(8,128)(2,1)} %w_hbm.1, ...), custom_call_target="tpu_custom_call" | custom-call | tf_op jit(solution)/shard_map/pallas_call | solution.py:418
  82.8 1.2 %slice_bitcast_fusion = f32[6]{0:T(128)} fusion(f32[8,128]{1,0:T(8,128)} %get-tuple-element.8), kind=kLoop, calls=%fused_computation | loop fusion | bytes 48 | tf_op jit(solution)/shard_map/squeeze | solution.py:435
  83.9 1.9 %copy.13 = f32[1,1024,128]{2,1,0:T(8,128)} copy(f32[1,1024,128]{2,1,0:T(8,128)} %bitcast.13) | data formatting | bytes 1048576
  85.8 1.9 %copy.14 = f32[1,1024,128]{2,1,0:T(8,128)} copy(f32[1,1024,128]{2,1,0:T(8,128)} %bitcast.12) | data formatting | bytes 1048576

commit v4 on v3

--- a/solution.py
+++ b/solution.py
@@ -90,8 +90,8 @@
             action(lax.rem(place + k, half))
 
     def send_inputs(chunk):
-        peer = lax.rem(place + 1 + chunk // 2, half)
-        if chunk % 2 == 0:
+        peer = lax.rem(place + 1 + chunk % (half - 1), half)
+        if chunk >= half - 1:
             source = first + peer
             half_copy(XOWN, x_hbm.at[:, columns(source)], xg.at[0, place], place, peer).start()
         else:
@@ -310,9 +310,8 @@
     tslots[me] = tpart[tspan(me), :]
     innerg[place] = inner[sec]
 
-    local[5].wait()
     local[6].wait()
-    for ex, ref in ((INNER, innerg), (XOWN, xg.at[0]), (XFAR, xg.at[1])):
+    for ex, ref in ((INNER, innerg), (XFAR, xg.at[1])):
         each_half(lambda peer: half_copy(ex, ref.at[peer], ref.at[peer], peer, peer).wait_recv())
     spread = innerg[...].reshape(half * rows, rank).T
     parts = cross.shape[0]
@@ -335,6 +334,10 @@
     def _(n):
         up_out[...] += mm(basis[n], tsum[tmat(n), :])
 
+    local[5].wait()
+    each_half(
+        lambda peer: half_copy(XOWN, xg.at[0, peer], xg.at[0, peer], peer, peer).wait_recv()
+    )
     for part in range(parts):
         held = xg[0, :, :, part * span : (part + 1) * span].reshape(half * rows, span)
         own = mm(spread, held)

time: 88 us -> 81.9 us (0.931)
  Pallas kernels: 80.8 us -> 74.5 us
    pallas_call x1, Pallas kernels: 80.8 us -> 74.5 us  [body(): pl.pallas_call(functools.partial(kernel, sections, peers, head_task.shape...]
where the time goes in v4:
time: 81.9 us; the launch traced here: 81.4 us
  Pallas kernels  74.5 us (91%)
  local copies, waits for them, and re-layouts  6.25 us (8%)
    pallas_call x1, Pallas kernels, body(): pl.pallas_call(functools.partial(kernel, sections, peers, head_task.shape...  74.5 us
    unnamed x3, local copies, waits for them, and re-layouts  5.06 us

profile of v4, /device:TPU:0, one launch (start us, length us, event | category | flops | bytes accessed | tf_op | source)
XLA Modules:
  0.0 81.4 jit_solution(4267441534960366211)
XLA Ops:
  0.6 1.3 %copy.10.head_task = s32[8,1]{1,0:T(8,128)} copy(s32[8,1]{0,1:T(1,128)} %param.13) | data formatting | bytes 64 | tf_op args[6]
  2.0 74.5 %shard_map.94 = (f32[1024,128]{1,0:T(8,128)}, f32[1024,128]{1,0:T(8,128)}, f32[8,128]{1,0:T(8,128)}) custom-call(bf16[128,8192]{1,0:T(8,128)(2,1)} %bitcast.9, bf16[8192,128]{1,0:T(8,128)(2,1)} %bitcast.10, bf16[8192,128]{1,0:T(8,128)(2,1)} %bitcast.11, bf16[32,8192]{1,0:T(8,128)(2,1)} %bitcast.14, bf16[1024,128]{1,0:T(8,128)(2,1)} %w_hbm.1, ...), custom_call_target="tpu_custom_call" | custom-call | tf_op jit(solution)/shard_map/pallas_call | solution.py:421
  76.4 1.2 %slice_bitcast_fusion = f32[6]{0:T(128)} fusion(f32[8,128]{1,0:T(8,128)} %get-tuple-element.8), kind=kLoop, calls=%fused_computation | loop fusion | bytes 48 | tf_op jit(solution)/shard_map/squeeze | solution.py:438
  77.6 1.9 %copy.13 = f32[1,1024,128]{2,1,0:T(8,128)} copy(f32[1,1024,128]{2,1,0:T(8,128)} %bitcast.13) | data formatting | bytes 1048576
  79.5 1.9 %copy.14 = f32[1,1024,128]{2,1,0:T(8,128)} copy(f32[1,1024,128]{2,1,0:T(8,128)} %bitcast.12) | data formatting | bytes 1048576
